TPU v7x, 32 devices: a whole 2x2x4 slice. The times are simulated.
32 devices in a mesh: slab: 4 (over y, x), kmom: 4 (over z), energy: 2 (over core).
Axes of the slice: x: 2, y: 2, z: 4, core: 2. Of those that a mesh axis runs over, the one named last changes fastest.
Arguments:
- free_green: float32 [4, 2, 4, 2, 256, 256], P('slab', 'energy', 'kmom'), as said below
- coupling: float32 [4, 256, 256], P('slab'), may hold values from -0.375 to 0.375
- coupling_tiles: int32 [4, 8, 3], P('slab'), may hold values from 0 to 7, as said below
- occupation: float32 [2], P('energy'), may hold values from 0.05 to 1
- phonon_weight: float32 [2, 4, 4], replicated, may hold values from 0.2 to 1
- phonon_mode: int32 [2], replicated, may hold values from 0 to 1, each once
Outputs:
- green: float32 [4, 2, 4, 2, 256, 256], P('slab', 'energy', 'kmom')
- self_energy: bfloat16 [4, 2, 4, 2, 256, 256], P('slab', 'energy', 'kmom')
Inputs may be any that keep to these rules, and one draw needn't show every extreme that they name: `coupling_tiles`: the 3 column tiles of one row tile are distinct. `phonon_mode`: each value once. `free_green`: the imaginary part of every diagonal entry is negative.
All inputs are finite; a program needn't handle non-finite values.
Results may differ from a plain program's by a relative error of at most 0.0034.
Values may be sent and summed in bfloat16 or wider, within the bound.
A program may use at most 64 MiB of HBM per device.

v0:
```python
import jax
import jax.numpy as jnp
from jax import lax
from jax.sharding import PartitionSpec as P


def passed_along(shard, axis, by):
    length = lax.axis_size(axis)
    pairs = [(i, i + by) for i in range(length) if 0 <= i + by < length]
    return lax.ppermute(shard, axis, pairs)


def extended_2(block, sides, width):
    for axis, dim in sides:
        count = lax.axis_size(axis)
        forward = [(i, i + 1) for i in range(count - 1)]
        backward = [(target, source) for source, target in forward]
        low = lax.ppermute(
            lax.slice_in_dim(block, block.shape[dim] - width, None, axis=dim), axis, forward
        )
        high = lax.ppermute(lax.slice_in_dim(block, 0, width, axis=dim), axis, backward)
        block = jnp.concatenate([low, block, high], axis=dim)
    return block


def complex_product(left_factor, right_factor):
    left_real = left_factor[..., 0, :, :]
    left_imag = left_factor[..., 1, :, :]
    right_real = right_factor[..., 0, :, :]
    right_imag = right_factor[..., 1, :, :]
    highest = lax.Precision.HIGHEST
    real_part = jnp.matmul(left_real, right_real, precision=highest) - jnp.matmul(
        left_imag, right_imag, precision=highest
    )
    imag_part = jnp.matmul(left_real, right_imag, precision=highest) + jnp.matmul(
        left_imag, right_real, precision=highest
    )
    return jnp.stack([real_part, imag_part], axis=-3)


def sandwich(pair_map, inner):
    return complex_product(complex_product(pair_map, inner), jnp.swapaxes(pair_map, -1, -2))


def on_device(free_green, coupling, coupling_tiles, occupation, phonon_weight, phonon_mode):
    slab_count = free_green.shape[0]
    block_width = coupling.shape[-1]
    tile_count = coupling_tiles.shape[1]
    tile_size = block_width // tile_count
    column_tile = jnp.arange(block_width, dtype=jnp.int32) // tile_size
    tile_hit = jnp.any(coupling_tiles[..., None] == column_tile, axis=-2).astype(jnp.float32)
    tile_mask = jnp.broadcast_to(
        tile_hit[:, :, None, :], (slab_count, tile_count, tile_size, block_width)
    ).reshape(slab_count, block_width, block_width)
    coupled = coupling * tile_mask
    pair_maps = [
        jnp.einsum("ekcij,jl->ekcil", free_green[0], coupled[0], precision=lax.Precision.HIGHEST)
    ]

    def sweep(beyond):
        current = beyond
        current = free_green[0] + sandwich(pair_maps[0], current)
        results = [current]
        return results[::-1]

    zero_block = jnp.zeros(free_green.shape[1:], jnp.float32)

    def advance(turn_index, beyond):
        first_green = sweep(beyond)[0]
        return passed_along(first_green, "slab", -1)

    beyond = lax.fori_loop(0, lax.axis_size("slab") - 1, advance, zero_block)
    green = jnp.stack(sweep(beyond))
    filling = occupation[None, :, None, None, None]
    real_part = -filling * (green[:, :, :, 0] - jnp.swapaxes(green[:, :, :, 0], -1, -2))
    imag_part = -filling * (green[:, :, :, 1] + jnp.swapaxes(green[:, :, :, 1], -1, -2))
    lesser = jnp.stack([real_part, imag_part], axis=3).astype(jnp.bfloat16)
    e_local = occupation.shape[0]
    k_local = green.shape[2]
    k_first = lax.axis_index("kmom") * k_local
    weights_mine = lax.dynamic_slice_in_dim(phonon_weight, k_first, k_local, 1)
    branch_count = phonon_weight.shape[0]
    gathered = lax.all_gather(lesser, "kmom", axis=2, tiled=True)
    mixed = jnp.einsum(
        "bkq,seqcij->bsekcij",
        weights_mine,
        gathered.astype(jnp.float32),
        precision=lax.Precision.HIGHEST,
    )
    extended = extended_2(mixed, (("energy", 2),), 1)
    self_energy = jnp.zeros(green.shape, jnp.float32)
    for branch in range(branch_count):
        self_energy = (
            self_energy
            + lax.dynamic_slice_in_dim(extended[branch], 1 + phonon_mode[branch], e_local, 1)
            + lax.dynamic_slice_in_dim(extended[branch], 1 - phonon_mode[branch], e_local, 1)
        )
    return (green, self_energy.astype(jnp.bfloat16))


def solution(mesh):
    in_specs = (
        P("slab", "energy", "kmom", None, None, None),
        P("slab", None, None),
        P("slab", None, None),
        P("energy"),
        P(),
        P(),
    )
    out_specs = (
        P("slab", "energy", "kmom", None, None, None),
        P("slab", "energy", "kmom", None, None, None),
    )
    return jax.shard_map(
        on_device, mesh=mesh, in_specs=in_specs, out_specs=out_specs, check_vma=False
    )
```

profile of v0, /device:TPU:1, one launch (start us, length us, event | category | flops | bytes accessed | tf_op | source)
XLA Modules:
  0.0 131.5 jit_solution(2320130267176986626)
XLA Ops:
  7.2 0.7 copy.50
  8.1 1.0 bitcast_multiply_fusion
  9.1 2.1 %fusion.26 = f32[256,2,256]{2,0,1:T(8,128)S(1)} fusion(f32[1,1,1,2,256,256]{5,4,3,2,1,0:T(8,128)} %param.8, f32[1,256,256]{2,1,0:T(8,128)S(1)} %bitcast_multiply_fusion), kind=kOutput, calls=%fused_computation.40 | convolution fusion | flops 402653184 | bytes 1310720 | tf_op jit(solution)/shard_map/ekcij,jl->ekcil/dot_general | solution.py:57
  11.5 53.8 %while.10 = (s32[]{:T(128)}, f32[1,1,2,256,256]{4,3,2,1,0:T(8,128)S(1)}, f32[1,1,1,2,256,256]{5,4,3,2,1,0:T(8,128)S(1)}, f32[1,1,2,256,256]{4,3,2,1,0:T(8,128)S(1)}, s32[]{:T(128)}) while((s32[]{:T(128)}, f32[1,1,2,256,256]{4,3,2,1,0:T(8,128)S(1)}, f32[1,1,1,2,256,256]{5,4,3,2,1,0:T(8,128)S(1)}, f32[1,1,2,256,256]{4,3,2,1,0:T(8,128)S(1)}, ...), condition=%wide.region_2.3_spmd, body=%wide.region_1.2_spmd.sunk | while | flops 1611137024 | bytes 11010149 | solution.py:72
  11.5 0.4 fusion.89
  11.9 0.4 fusion.91
  12.2 0.4 convolution_subtract_fusion.5
  12.6 0.4 fusion.90
  13.1 0.4 fusion.93
  13.5 0.4 convolution_add_fusion.5
  13.9 0.4 fusion.92
  14.3 0.4 fusion.94
  14.8 1.3 collective-permute-start
  16.1 14.3 %collective-permute-done = f32[1,1,2,256,256]{4,3,2,1,0:T(8,128)S(1)} collective-permute-done((f32[1,1,2,256,256]{4,3,2,1,0:T(8,128)S(1)}, f32[1,1,2,256,256]{4,3,2,1,0:T(8,128)S(1)}, u32[]{:S(2)}, u32[]{:S(2)}) %collective-permute-start) | collective-permute-done | bytes 524320 | tf_op jit(solution)/shard_map/while/body/eval_jaxpr/ppermute | solution.py:10
  31.1 0.4 convolution_subtract_fusion.5
  31.5 0.4 fusion.90
  31.9 0.4 fusion.93
  32.4 0.4 convolution_add_fusion.5
  32.7 0.4 fusion.92
  33.2 0.4 fusion.94
  33.7 1.3 collective-permute-start
  35.0 13.3 %collective-permute-done = f32[1,1,2,256,256]{4,3,2,1,0:T(8,128)S(1)} collective-permute-done((f32[1,1,2,256,256]{4,3,2,1,0:T(8,128)S(1)}, f32[1,1,2,256,256]{4,3,2,1,0:T(8,128)S(1)}, u32[]{:S(2)}, u32[]{:S(2)}) %collective-permute-start) | collective-permute-done | bytes 524320 | tf_op jit(solution)/shard_map/while/body/eval_jaxpr/ppermute | solution.py:10
  48.7 0.4 fusion.91
  49.0 0.4 convolution_subtract_fusion.5
  49.4 0.4 fusion.90
  49.9 0.4 fusion.93
  50.3 0.4 convolution_add_fusion.5
  50.7 0.4 fusion.92
  51.1 0.4 fusion.94
  51.6 1.3 collective-permute-start
  52.9 12.4 %collective-permute-done = f32[1,1,2,256,256]{4,3,2,1,0:T(8,128)S(1)} collective-permute-done((f32[1,1,2,256,256]{4,3,2,1,0:T(8,128)S(1)}, f32[1,1,2,256,256]{4,3,2,1,0:T(8,128)S(1)}, u32[]{:S(2)}, u32[]{:S(2)}) %collective-permute-start) | collective-permute-done | bytes 524320 | tf_op jit(solution)/shard_map/while/body/eval_jaxpr/ppermute | solution.py:10
  65.3 0.6 fusion.37
  65.9 0.6 fusion.33
  66.5 0.6 convolution_subtract_fusion.3
  67.1 0.4 fusion.39
  67.9 0.6 convolution_add_fusion.3
  68.5 0.4 fusion.23
  68.9 0.4 fusion.22
  70.6 0.7 maximum_bitcast_fusion
  71.3 31.8 %all-gather.2.cloned.1.call-done = bf16[1,1,4,2,256,256]{5,4,3,1,0,2:T(8,128)(2,1)} async-done(((bf16[1,1,1,2,256,256]{5,4,3,1,0,2:T(8,128)(2,1)}), bf16[1,1,4,2,256,256]{5,4,3,1,0,2:T(8,128)(2,1)}) %all-gather.2.cloned.1.call-update) | async-done | bytes 1048592 | tf_op jit(solution)/shard_map/all_gather | solution.py:83
  103.2 3.2 %convolution_bitcast_fusion = f32[2,1,1,1,2,256,256]{6,0,5,4,3,2,1:T(2,128)S(1)} fusion(f32[2,4,1,1]{1,0,3,2:T(2,128)S(1)} %bitcast.202, bf16[1,1,4,2,256,256]{5,4,3,1,0,2:T(8,128)(2,1)} %all-gather.2.cloned.1.call-done), kind=kOutput, calls=%fused_computation.30 | convolution fusion | flops 12582912 | bytes 2097184 | tf_op jit(solution)/shard_map/bkq,seqcij->bsekcij/dot_general | solution.py:84
  106.4 1.3 collective-permute-start.1
  107.7 4.1 %collective-permute-start.2 = (f32[2,1,1,1,2,256,256]{6,0,5,4,3,2,1:T(2,128)S(1)}, f32[2,1,1,1,2,256,256]{6,0,5,4,3,2,1:T(2,128)}, u32[]{:S(2)}, u32[]{:S(2)}) collective-permute-start(f32[2,1,1,1,2,256,256]{6,0,5,4,3,2,1:T(2,128)S(1)} %convolution_bitcast_fusion), channel_id=1, source_target_pairs={{1,0},{3,2},{5,4},{7,6},{9,8},{11,10},{13,12},{15,14},{17,16},{19,... | collective-permute-start | bytes 3145736 | tf_op jit(solution)/shard_map/ppermute | solution.py:21
  111.8 0.6 fusion.49
  117.2 3.0 %pad_maximum_fusion = f32[2,1,3,1,2,256,256]{6,0,5,4,3,2,1:T(2,128)S(1)} fusion(f32[2,1,1,1,2,256,256]{6,0,5,4,3,2,1:T(2,128)} %collective-permute-done.2, f32[2,1,1,1,2,256,256]{6,0,5,4,3,2,1:T(2,128)S(1)} %convolution_bitcast_fusion, f32[2,1,1,1,2,256,256]{6,0,5,4,3,2,1:T(2,128)S(1)} %collective-permute-done.1), kind=kLoop, calls=%fused_computation.29 | loop fusion | flops 1572864 | bytes 6291456 | tf_op jit(solution)/shard_map/concatenate | solution.py:22
  120.3 2.7 %fusion.47 = (f32[1,1,3,1,2,256,256]{6,0,5,4,3,2,1:T(1,128)S(1)}, f32[1,1,3,1,2,256,256]{6,0,5,4,3,2,1:T(1,128)S(1)}) fusion(f32[2,1,3,1,2,256,256]{6,0,5,4,3,2,1:T(2,128)S(1)} %pad_maximum_fusion), kind=kLoop, calls=%fused_computation.79 | loop fusion | bytes 6291456 | tf_op jit(solution)/shard_map/slice | solution.py:95
  123.0 0.9 add_convert_fusion
  123.9 0.7 copy.49
  (32 shorter events, 2.7 us)
Async XLA Ops:
  7.2 64.2 %copy-start = (f32[2,4,4]{2,1,0:T(4,128)S(1)}, f32[2,4,4]{2,1,0:T(4,128)}, u32[]{:S(2)}) copy-start(f32[2,4,4]{2,1,0:T(4,128)} %param.12) | copy-start | bytes 388
  7.2 4.3 %copy-start.1 = (f32[1,1,1,2,256,256]{5,4,3,2,1,0:T(8,128)S(1)}, f32[1,1,1,2,256,256]{5,4,3,2,1,0:T(8,128)}, u32[]{:S(2)}) copy-start(f32[1,1,1,2,256,256]{5,4,3,2,1,0:T(8,128)} %param.8) | copy-start | bytes 1572868
  7.2 96.0 %all-gather.2.cloned.1.call-start = ((), (), s32[]{:S(2)}) async-start(), calls=%async_computation | async-start | bytes 1310720 | tf_op jit(solution)/shard_map/all_gather | solution.py:83
  14.8 15.6 %collective-permute-start = (f32[1,1,2,256,256]{4,3,2,1,0:T(8,128)S(1)}, f32[1,1,2,256,256]{4,3,2,1,0:T(8,128)S(1)}, u32[]{:S(2)}, u32[]{:S(2)}) collective-permute-start(f32[1,1,2,256,256]{4,3,2,1,0:T(8,128)S(1)} %maximum_add_fusion.3), channel_id=1, source_target_pairs={{8,0},{16,8},{24,16},{9,1},{17,9},{25,17},{10,2},{18,10},{26,18},{... | collective-permute-start | bytes 1572872 | tf_op jit(solution)/shard_map/while/body/eval_jaxpr/ppermute | solution.py:10
  33.7 14.6 %collective-permute-start = (f32[1,1,2,256,256]{4,3,2,1,0:T(8,128)S(1)}, f32[1,1,2,256,256]{4,3,2,1,0:T(8,128)S(1)}, u32[]{:S(2)}, u32[]{:S(2)}) collective-permute-start(f32[1,1,2,256,256]{4,3,2,1,0:T(8,128)S(1)} %maximum_add_fusion.3), channel_id=1, source_target_pairs={{8,0},{16,8},{24,16},{9,1},{17,9},{25,17},{10,2},{18,10},{26,18},{... | collective-permute-start | bytes 1572872 | tf_op jit(solution)/shard_map/while/body/eval_jaxpr/ppermute | solution.py:10
  51.6 13.7 %collective-permute-start = (f32[1,1,2,256,256]{4,3,2,1,0:T(8,128)S(1)}, f32[1,1,2,256,256]{4,3,2,1,0:T(8,128)S(1)}, u32[]{:S(2)}, u32[]{:S(2)}) collective-permute-start(f32[1,1,2,256,256]{4,3,2,1,0:T(8,128)S(1)} %maximum_add_fusion.3), channel_id=1, source_target_pairs={{8,0},{16,8},{24,16},{9,1},{17,9},{25,17},{10,2},{18,10},{26,18},{... | collective-permute-start | bytes 1572872 | tf_op jit(solution)/shard_map/while/body/eval_jaxpr/ppermute | solution.py:10
  69.3 37.0 %copy-start.2 = (f32[1,1,1,2,256,256]{5,4,3,2,1,0:T(8,128)}, f32[1,1,1,2,256,256]{5,4,3,2,1,0:T(8,128)S(1)}, u32[]{:S(2)}) copy-start(f32[1,1,1,2,256,256]{5,4,3,2,1,0:T(8,128)S(1)} %maximum_add_fusion.1) | copy-start | bytes 1572868
  69.8 42.0 %copy-start.3 = (s32[2]{0:T(128)S(1)}, s32[2]{0:T(128)}, u32[]{:S(2)}) copy-start(s32[2]{0:T(128)} %param.13) | copy-start | bytes 28
  106.4 10.8 %collective-permute-start.1 = (f32[2,1,1,1,2,256,256]{6,0,5,4,3,2,1:T(2,128)S(1)}, f32[2,1,1,1,2,256,256]{6,0,5,4,3,2,1:T(2,128)S(1)}, u32[]{:S(2)}, u32[]{:S(2)}) collective-permute-start(f32[2,1,1,1,2,256,256]{6,0,5,4,3,2,1:T(2,128)S(1)} %convolution_bitcast_fusion), channel_id=1, source_target_pairs={{0,1},{2,3},{4,5},{6,7},{8,9},{10,11},{12,13},{14,15},{16,17},{18,... | collective-permute-start | bytes 3145736 | tf_op jit(solution)/shard_map/ppermute | solution.py:18
  107.7 9.5 %collective-permute-start.2 = (f32[2,1,1,1,2,256,256]{6,0,5,4,3,2,1:T(2,128)S(1)}, f32[2,1,1,1,2,256,256]{6,0,5,4,3,2,1:T(2,128)}, u32[]{:S(2)}, u32[]{:S(2)}) collective-permute-start(f32[2,1,1,1,2,256,256]{6,0,5,4,3,2,1:T(2,128)S(1)} %convolution_bitcast_fusion), channel_id=1, source_target_pairs={{1,0},{3,2},{5,4},{7,6},{9,8},{11,10},{13,12},{15,14},{17,16},{19,... | collective-permute-start | bytes 3145736 | tf_op jit(solution)/shard_map/ppermute | solution.py:21
Sparse Core Ops, SparseCore 0:
  71.4 31.6 all-gather.1
where the time goes:
time: 132 us
  waiting for transfers between devices  71.9 us (54%)
  between operations  19.8 us (15%)
  matrix products  18.7 us (14%)
  starting transfers between devices  9.28 us (7%)
  other arithmetic  6.12 us (5%)
  local copies, waits for them, and re-layouts  5.45 us (4%)
    ppermute x3, waiting for transfers between devices, passed_along(): return lax.ppermute(shard, axis, pairs)  40 us
    all_gather x1, waiting for transfers between devices, on_device(): gathered = lax.all_gather(lesser, 'kmom', axis=2, tiled=True)  31.8 us
    ppermute x1, starting transfers between devices, extended_2(): lax.ppermute(lax.slice_in_dim(block, 0, width, axis=dim), axis, backward)  4.08 us
    ppermute x3, starting transfers between devices, passed_along(): return lax.ppermute(shard, axis, pairs)  3.88 us
    dot_general x8, matrix products, complex_product(): jnp.matmul(left_imag, right_imag, precision=highest)  3.36 us
    dot_general x8, matrix products, complex_product(): jnp.matmul(left_imag, right_real, precision=highest)  3.35 us
    dot_general x8, matrix products, complex_product(): jnp.matmul(left_real, right_imag, precision=highest)  3.34 us
    dot_general x8, matrix products, complex_product(): jnp.matmul(left_real, right_real, precision=highest)  3.34 us
  transfers between devices with their start and end apart: 6, of which 4 were waited for; matrix products, arithmetic and copies ran while one was open for 0% of the time, Pallas kernels for 0%

commit v1 on v0

v1 whole, which is shorter than its diff:
```python
import functools

import jax
import jax.numpy as jnp
from jax import lax
from jax.experimental import pallas as pl
from jax.experimental.pallas import tpu as pltpu
from jax.sharding import PartitionSpec as P

F32 = jnp.float32
BF16 = jnp.bfloat16
CHUNKS = 2


def mm(a, b):
    return jnp.dot(a, b, preferred_element_type=F32)


def split(x):
    high = x.astype(BF16)
    return high, (x - high.astype(F32)).astype(BF16)


def fold(products, nb):
    return (
        products[:nb, :nb] - products[nb:, nb:],
        products[:nb, nb:] + products[nb:, :nb],
    )


def remote(src, dst, send_sem, recv_sem, **where):
    return pltpu.make_async_remote_copy(
        src_ref=src,
        dst_ref=dst,
        send_sem=send_sem,
        recv_sem=recv_sem,
        device_id=where,
        device_id_type=pl.DeviceIdType.MESH,
    )


def kernel(
    sizes, g_hbm, c_hbm, tiles, occ, weight, mode, green_hbm, self_hbm,
    a_ref, c_ref, qh, ql, qth, qtl, send_a, send_q, got_a, got_q,
    packed, sum0, sum1, near, out_ref,
    in_sem, out_sem, sa_sem, sq_sem, ra_sem, rq_sem,
    right_sem, left_sem, block_sem, es_sem, er_sem,
):
    slabs, momenta, energies, levels = sizes
    nb = c_ref.shape[0]
    j = lax.axis_index("slab")
    k = lax.axis_index("kmom")
    e = lax.axis_index("energy")

    load_g = pltpu.make_async_copy(g_hbm, a_ref, in_sem.at[0])
    load_c = pltpu.make_async_copy(c_hbm, c_ref, in_sem.at[1])
    load_g.start()
    load_c.start()

    barrier = pltpu.get_barrier_semaphore()

    def greet(**where):
        pl.semaphore_signal(
            barrier, inc=1, device_id=where, device_id_type=pl.DeviceIdType.MESH
        )

    for step in range(1, slabs):
        greet(slab=lax.rem(j + step, slabs))
    pl.when(k > 0)(lambda: greet(kmom=k - 1))
    pl.when(k < momenta - 1)(lambda: greet(kmom=k + 1))
    pl.when(e > 0)(lambda: greet(energy=e - 1))
    pl.when(e < energies - 1)(lambda: greet(energy=e + 1))

    load_g.wait()

    def pack_for_send(buffer):
        buffer[:, :nb] = a_ref[:nb, :].astype(BF16)
        buffer[:, nb:] = a_ref[nb:, :].astype(BF16)

    peers = slabs - 1
    for there in (k > 0, k < momenta - 1, e > 0, e < energies - 1):
        peers += jnp.where(there, 1, 0)
    pl.semaphore_wait(barrier, peers)

    def a_copy(level, to):
        return remote(
            send_a, got_a.at[level], sa_sem.at[to], ra_sem.at[level],
            slab=lax.max(j - 1 - to, 0),
        )

    def q_copy(level, to):
        return remote(
            send_q, got_q.at[level], sq_sem.at[to], rq_sem.at[level],
            slab=lax.max(j - 1 - to, 0),
        )

    def roles(level):
        half = 1 << level
        base = (j // (2 * half)) * (2 * half)
        sender = lax.rem(j, 2 * half) == half
        receiver = jnp.logical_and(lax.rem(j, 2 * half) < half, base + half < slabs)
        with_q = base + 2 * half < slabs
        return half, sender, receiver, with_q

    def send_own_a(level):
        pack_for_send(send_a)
        for to in range(1 << level):
            a_copy(level, to).start()

    pl.when(roles(0)[1])(lambda: send_own_a(0))

    load_c.wait()

    def set_q(q):
        high, low = split(q)
        qh[...] = high
        ql[...] = low
        high, low = split(q.T)
        qth[...] = high
        qtl[...] = low

    @pl.when(j < slabs - 1)
    def _():
        gh, gl = split(a_ref[...])
        size = nb // tiles.shape[1]
        parts = []
        column = lax.broadcasted_iota(jnp.int32, (size, nb), 1) // size
        for row in range(tiles.shape[1]):
            hit = column == tiles[0, row, 0]
            for other in range(1, tiles.shape[2]):
                hit = jnp.logical_or(hit, column == tiles[0, row, other])
            rows = pl.ds(row * size, size)
            parts.append(jnp.where(hit, c_ref[rows, :], 0.0))
        ch, cl = split(jnp.concatenate(parts, axis=0))
        set_q(mm(gh, ch) + mm(gl, ch) + mm(gh, cl))

    for level in range(levels):
        half, sender, receiver, with_q = roles(level)

        @pl.when(sender)
        def _():
            if level > 0:
                send_own_a(level)

            @pl.when(with_q)
            def _():
                send_q[:, :nb] = qh[:nb, :]
                send_q[:, nb:] = qh[nb:, :]
                for to in range(half):
                    q_copy(level, to).start()

        @pl.when(receiver)
        def _():
            a_copy(level, 0).wait_recv()
            beyond = got_a[level]
            t_real, t_imag = fold(mm(qh[...], beyond) + mm(ql[...], beyond), nb)
            th, tl = split(jnp.concatenate([t_real, t_imag], axis=0))
            real, imag = fold(mm(th, qth[...]) + mm(tl, qth[...]) + mm(th, qtl[...]), nb)
            a_ref[:nb, :] += real
            a_ref[nb:, :] += imag

            @pl.when(with_q)
            def _():
                q_copy(level, 0).wait_recv()
                later = got_q[level]
                q_real, q_imag = fold(mm(qh[...], later) + mm(ql[...], later), nb)
                set_q(jnp.concatenate([q_real, q_imag], axis=0))

    store_green = pltpu.make_async_copy(a_ref, green_hbm, out_sem.at[0])
    store_green.start()

    row = lax.broadcasted_iota(jnp.int32, (nb, nb), 0)
    col = lax.broadcasted_iota(jnp.int32, (nb, nb), 1)
    real, imag = a_ref[:nb, :], a_ref[nb:, :]
    mirrored = jnp.where(col < row, -real, imag).T
    packed[k] = (-occ[0] * (jnp.where(col > row, real, imag) + mirrored)).astype(BF16)

    rows_of = [pl.ds(c * (nb // CHUNKS), nb // CHUNKS) for c in range(CHUNKS)]

    def to_right(q, c):
        block = packed.at[q, rows_of[c]]
        return remote(
            block, block, right_sem.at[q, c], block_sem.at[q, c],
            kmom=lax.min(k + 1, momenta - 1),
        )

    def to_left(q, c):
        block = packed.at[q, rows_of[c]]
        return remote(
            block, block, left_sem.at[q, c], block_sem.at[q, c], kmom=lax.max(k - 1, 0)
        )

    def near_copy(side, c):
        target = lax.min(e + 1, energies - 1) if side == 0 else lax.max(e - 1, 0)
        return remote(
            sum1.at[rows_of[c]], near.at[side, rows_of[c]],
            es_sem.at[side, c], er_sem.at[side, c], energy=target,
        )

    has_right, has_left = k < momenta - 1, k > 0
    has_next, has_before = e < energies - 1, e > 0

    for c in range(CHUNKS):
        pl.when(has_right)(lambda: to_right(k, c).start())
        pl.when(has_left)(lambda: to_left(k, c).start())

    def weights(q):
        w0, w1 = jnp.float32(0), jnp.float32(0)
        for branch in range(weight.shape[0]):
            value = weight[branch, k, q]
            w0 += jnp.where(mode[branch] == 0, 2.0 * value, 0.0)
            w1 += jnp.where(mode[branch] == 0, 0.0, value)
        return w0, w1

    own0, own1 = weights(k)
    for c in range(CHUNKS):
        block = packed[k, rows_of[c]].astype(F32)
        sum0[rows_of[c]] = own0 * block
        sum1[rows_of[c]] = own1 * block

    def take(q, c):
        w0, w1 = weights(q)
        block = packed[q, rows_of[c]].astype(F32)
        sum1[rows_of[c]] += w1 * block
        sum0[rows_of[c]] += w0 * block

    for step in range(1, momenta):
        low, high = k - step, k + step
        for c in range(CHUNKS):

            @pl.when(low >= 0)
            def _():
                q = lax.max(low, 0)
                to_right(q, c).wait_recv()
                pl.when(has_right)(lambda: to_right(q, c).start())

            @pl.when(high < momenta)
            def _():
                q = lax.min(high, momenta - 1)
                to_left(q, c).wait_recv()
                pl.when(has_left)(lambda: to_left(q, c).start())

            pl.when(low >= 0)(lambda: take(lax.max(low, 0), c))
            pl.when(high < momenta)(lambda: take(lax.min(high, momenta - 1), c))
            if step == momenta - 1:
                pl.when(has_next)(lambda: near_copy(0, c).start())
                pl.when(has_before)(lambda: near_copy(1, c).start())
    if momenta == 1:
        for c in range(CHUNKS):
            pl.when(has_next)(lambda: near_copy(0, c).start())
            pl.when(has_before)(lambda: near_copy(1, c).start())

    for c in range(CHUNKS):

        @pl.when(has_before)
        def _():
            near_copy(0, c).wait_recv()
            sum0[rows_of[c]] += near[0, rows_of[c]]

        @pl.when(has_next)
        def _():
            near_copy(1, c).wait_recv()
            sum0[rows_of[c]] += near[1, rows_of[c]]

    total = sum0[...]
    turned = total.T
    out_ref[:nb, :] = jnp.where(
        col > row, total, jnp.where(col < row, -turned, 0.0)
    ).astype(BF16)
    out_ref[nb:, :] = jnp.where(row >= col, total, turned).astype(BF16)
    store_self = pltpu.make_async_copy(out_ref, self_hbm, out_sem.at[1])
    store_self.start()

    for level in range(levels):
        half, sender, receiver, with_q = roles(level)

        @pl.when(sender)
        def _():
            for to in range(half):
                a_copy(level, to).wait_send()

            @pl.when(with_q)
            def _():
                for to in range(half):
                    q_copy(level, to).wait_send()

    for c in range(CHUNKS):
        for q in range(momenta):
            pl.when(jnp.logical_and(has_right, q <= k))(
                lambda: to_right(q, c).wait_send()
            )
            pl.when(jnp.logical_and(has_left, q >= k))(lambda: to_left(q, c).wait_send())
        pl.when(has_next)(lambda: near_copy(0, c).wait_send())
        pl.when(has_before)(lambda: near_copy(1, c).wait_send())
    store_green.wait()
    store_self.wait()


def on_device(free_green, coupling, coupling_tiles, occupation, phonon_weight, phonon_mode):
    slabs = lax.axis_size("slab")
    momenta = lax.axis_size("kmom")
    energies = lax.axis_size("energy")
    nb = coupling.shape[-1]
    levels = max((slabs - 1).bit_length(), 1)
    most = 1 << (levels - 1)
    smem = pl.BlockSpec(memory_space=pltpu.SMEM)
    hbm = pl.BlockSpec(memory_space=pltpu.HBM)
    dma = pltpu.SemaphoreType.DMA
    green, self_energy = pl.pallas_call(
        functools.partial(kernel, (slabs, momenta, energies, levels)),
        out_shape=(
            jax.ShapeDtypeStruct((2 * nb, nb), F32),
            jax.ShapeDtypeStruct((2 * nb, nb), BF16),
        ),
        in_specs=[hbm, hbm, smem, smem, smem, smem],
        out_specs=(hbm, hbm),
        scratch_shapes=[
            pltpu.VMEM((2 * nb, nb), F32),
            pltpu.VMEM((nb, nb), F32),
            pltpu.VMEM((2 * nb, nb), BF16),
            pltpu.VMEM((2 * nb, nb), BF16),
            pltpu.VMEM((nb, 2 * nb), BF16),
            pltpu.VMEM((nb, 2 * nb), BF16),
            pltpu.VMEM((nb, 2 * nb), BF16),
            pltpu.VMEM((nb, 2 * nb), BF16),
            pltpu.VMEM((levels, nb, 2 * nb), BF16),
            pltpu.VMEM((levels, nb, 2 * nb), BF16),
            pltpu.VMEM((momenta, nb, nb), BF16),
            pltpu.VMEM((nb, nb), F32),
            pltpu.VMEM((nb, nb), F32),
            pltpu.VMEM((2, nb, nb), F32),
            pltpu.VMEM((2 * nb, nb), BF16),
            dma((2,)),
            dma((2,)),
            dma((most,)),
            dma((most,)),
            dma((levels,)),
            dma((levels,)),
            dma((momenta, CHUNKS)),
            dma((momenta, CHUNKS)),
            dma((momenta, CHUNKS)),
            dma((2, CHUNKS)),
            dma((2, CHUNKS)),
        ],
        compiler_params=pltpu.CompilerParams(
            collective_id=0, has_side_effects=True, vmem_limit_bytes=40 * 1024 * 1024
        ),
    )(
        free_green.reshape(2 * nb, nb),
        coupling.reshape(nb, nb),
        coupling_tiles,
        occupation,
        phonon_weight,
        phonon_mode,
    )
    return green.reshape(free_green.shape), self_energy.reshape(free_green.shape)


def solution(mesh):
    in_specs = (
        P("slab", "energy", "kmom", None, None, None),
        P("slab", None, None),
        P("slab", None, None),
        P("energy"),
        P(),
        P(),
    )
    out_specs = (
        P("slab", "energy", "kmom", None, None, None),
        P("slab", "energy", "kmom", None, None, None),
    )
    return jax.shard_map(
        on_device, mesh=mesh, in_specs=in_specs, out_specs=out_specs, check_vma=False
    )
```

time: 132 us -> 41.4 us (0.31)
  waiting for transfers between devices: 71.9 us -> 0 us
  Pallas kernels: 0 us -> 35 us
  matrix products: 18.7 us -> 0 us
  between operations: 19.8 us -> 1.31 us
  starting transfers between devices: 9.28 us -> 0 us
  other arithmetic: 6.12 us -> 0 us
    ppermute x5 -> x0, waiting for transfers between devices: 40 us -> none  [the longest x3 40 us: passed_along(): return lax.ppermute(shard, axis, pairs)]
    pallas_call x0 -> x1, Pallas kernels: none -> 35 us  [on_device(): pl.pallas_call(functools.partial(kernel, (slabs, momenta, energies, level...]
    all_gather x1 -> x0, waiting for transfers between devices: 31.8 us -> none  [on_device(): gathered = lax.all_gather(lesser, 'kmom', axis=2, tiled=True)]
    dot_general x34 -> x0, matrix products: 18.7 us -> none  [the longest x8 3.36 us: complex_product(): jnp.matmul(left_imag, right_imag, precision=highest)]
    ppermute x5 -> x0, starting transfers between devices: 9.24 us -> none  [the longest x1 4.08 us: extended_2(): lax.ppermute(lax.slice_in_dim(block, 0, width, axis=dim), axis, backward)]
    slice x3 -> x0, local copies, waits for them, and re-layouts: 3.3 us -> none  [the longest x1 2.69 us: on_device(): extended[branch]]
    unnamed x11 -> x13, local copies, waits for them, and re-layouts: 1.63 us -> 4.81 us
    concatenate x1 -> x0, other arithmetic: 3.05 us -> none  [extended_2(): block = jnp.concatenate([low, block, high], axis=dim)]
  transfers between devices with their start and end apart: 6 -> 0, of which waited for: 4 -> 0; matrix products, arithmetic and copies ran while one was open for 0% -> 0% of each run, Pallas kernels for 0% -> 0%
where the time goes in v1:
time: 41.4 us; the launch traced here: 41.1 us
  Pallas kernels  35 us (85%)
  local copies, waits for them, and re-layouts  4.81 us (12%)
  between operations  1.31 us (3%)
    pallas_call x1, Pallas kernels, on_device(): pl.pallas_call(functools.partial(kernel, (slabs, momenta, energies, level...  35 us
    unnamed x13, local copies, waits for them, and re-layouts  4.81 us

profile of v1, /device:TPU:1, one launch (start us, length us, event | category | flops | bytes accessed | tf_op | source)
XLA Modules:
  0.0 41.1 jit_solution(6344623852445284883)
XLA Ops:
  1.3 0.0 copy-start.4
  1.3 0.0 copy-start.2
  1.3 0.7 %copy-done.4 = s32[1,8,3]{1,0,2:T(1,128)S(1)} copy-done((s32[1,8,3]{1,0,2:T(1,128)S(1)}, s32[1,8,3]{1,0,2:T(1,128)}, u32[]{:S(2)}) %copy-start.4) | copy-done | bytes 120
  2.0 0.0 copy-start.3
  2.0 0.1 copy.8.tiles
  2.0 0.0 copy-done.2
  2.0 0.6 %copy-done.3 = s32[2]{0:T(128)S(1)} copy-done((s32[2]{0:T(128)S(1)}, s32[2]{0:T(128)}, u32[]{:S(2)}) %copy-start.3) | copy-done | bytes 32
  2.6 0.0 copy-start
  2.6 1.0 %copy-done = f32[1,1,1,2,256,256]{5,4,3,2,1,0:T(8,128)S(1)} copy-done((f32[1,1,1,2,256,256]{5,4,3,2,1,0:T(8,128)S(1)}, f32[1,1,1,2,256,256]{5,4,3,2,1,0:T(8,128)}, u32[]{:S(2)}) %copy-start) | copy-done | bytes 524312
  3.7 0.0 copy-start.1
  3.7 0.9 %copy-done.1 = f32[1,256,256]{2,1,0:T(8,128)S(1)} copy-done((f32[1,256,256]{2,1,0:T(8,128)S(1)}, f32[1,256,256]{2,1,0:T(8,128)}, u32[]{:S(2)}) %copy-start.1) | copy-done | bytes 262168
  4.6 35.0 %shard_map.77 = (f32[512,256]{1,0:T(8,128)S(1)}, bf16[512,256]{1,0:T(8,128)(2,1)S(1)}) custom-call(f32[512,256]{1,0:T(8,128)S(1)} %bitcast.4, f32[256,256]{1,0:T(8,128)S(1)} %bitcast.6, s32[1,8,3]{2,1,0:T(8,128)S(1)} %copy.8.tiles, f32[1]{0:T(128)S(6)} %copy.11.occ, f32[2,4,4]{2,1,0:T(4,128)S(1)} %copy-done.2, s32[2]{0:T(128)S(1)} %copy-done.3), custom_call_target="tpu_custom_call" | custom-call | tf_op jit(solution)/shard_map/pallas_call | solution.py:309
  39.6 0.8 %copy.12 = f32[1,1,1,2,256,256]{5,4,3,2,1,0:T(8,128)} copy(f32[1,1,1,2,256,256]{5,4,3,2,1,0:T(8,128)S(1)} %bitcast.5) | data formatting | bytes 1048576
  40.4 0.7 %copy.13 = bf16[1,1,1,2,256,256]{5,4,3,2,1,0:T(8,128)(2,1)} copy(bf16[1,1,1,2,256,256]{5,4,3,2,1,0:T(8,128)(2,1)S(1)} %bitcast.7) | data formatting | bytes 524288
Async XLA Ops:
  1.3 0.7 %copy-start.4 = (s32[1,8,3]{1,0,2:T(1,128)S(1)}, s32[1,8,3]{1,0,2:T(1,128)}, u32[]{:S(2)}) copy-start(s32[1,8,3]{1,0,2:T(1,128)} %param.8) | copy-start | bytes 292
  1.3 0.8 %copy-start.2 = (f32[2,4,4]{2,1,0:T(4,128)S(1)}, f32[2,4,4]{2,1,0:T(4,128)}, u32[]{:S(2)}) copy-start(f32[2,4,4]{2,1,0:T(4,128)} %weight.1) | copy-start | bytes 388
  2.0 0.7 %copy-start.3 = (s32[2]{0:T(128)S(1)}, s32[2]{0:T(128)}, u32[]{:S(2)}) copy-start(s32[2]{0:T(128)} %mode.1) | copy-start | bytes 28
  2.6 1.0 %copy-start = (f32[1,1,1,2,256,256]{5,4,3,2,1,0:T(8,128)S(1)}, f32[1,1,1,2,256,256]{5,4,3,2,1,0:T(8,128)}, u32[]{:S(2)}) copy-start(f32[1,1,1,2,256,256]{5,4,3,2,1,0:T(8,128)} %param.6) | copy-start | bytes 1572868
  3.7 0.9 %copy-start.1 = (f32[1,256,256]{2,1,0:T(8,128)S(1)}, f32[1,256,256]{2,1,0:T(8,128)}, u32[]{:S(2)}) copy-start(f32[1,256,256]{2,1,0:T(8,128)} %param.7) | copy-start | bytes 786436

commit v2 on v1

--- a/solution.py
+++ b/solution.py
@@ -10,6 +10,7 @@
 F32 = jnp.float32
 BF16 = jnp.bfloat16
 CHUNKS = 2
+VMEM_BYTES = 62 * 1024 * 1024
 
 
 def mm(a, b):
@@ -40,8 +41,8 @@
 
 
 def kernel(
-    sizes, g_hbm, c_hbm, tiles, occ, weight, mode, green_hbm, self_hbm,
-    a_ref, c_ref, qh, ql, qth, qtl, send_a, send_q, got_a, got_q,
+    sizes, g_hbm, c_hbm, tiles_hbm, occ_hbm, weight_hbm, mode_hbm, green_hbm, self_hbm,
+    tiles, occ, weight, mode, a_ref, c_ref, qh, ql, qth, qtl, send_a, send_q, got_a, got_q,
     packed, sum0, sum1, near, out_ref,
     in_sem, out_sem, sa_sem, sq_sem, ra_sem, rq_sem,
     right_sem, left_sem, block_sem, es_sem, er_sem,
@@ -56,6 +57,14 @@
     load_c = pltpu.make_async_copy(c_hbm, c_ref, in_sem.at[1])
     load_g.start()
     load_c.start()
+    small_loads = [
+        pltpu.make_async_copy(source, target, in_sem.at[2 + index])
+        for index, (source, target) in enumerate(
+            ((tiles_hbm, tiles), (occ_hbm, occ), (weight_hbm, weight), (mode_hbm, mode))
+        )
+    ]
+    for load in small_loads:
+        load.start()
 
     barrier = pltpu.get_barrier_semaphore()
 
@@ -73,19 +82,18 @@
 
     load_g.wait()
 
-    def pack_for_send(buffer):
-        buffer[:, :nb] = a_ref[:nb, :].astype(BF16)
-        buffer[:, nb:] = a_ref[nb:, :].astype(BF16)
+    rows_of = [pl.ds(c * (nb // CHUNKS), nb // CHUNKS) for c in range(CHUNKS)]
+    imag_rows_of = [pl.ds(nb + c * (nb // CHUNKS), nb // CHUNKS) for c in range(CHUNKS)]
 
     peers = slabs - 1
     for there in (k > 0, k < momenta - 1, e > 0, e < energies - 1):
         peers += jnp.where(there, 1, 0)
     pl.semaphore_wait(barrier, peers)
 
-    def a_copy(level, to):
-        return remote(
-            send_a, got_a.at[level], sa_sem.at[to], ra_sem.at[level],
-            slab=lax.max(j - 1 - to, 0),
+    def a_copy(level, to, c):
+        return remote(
+            send_a.at[rows_of[c]], got_a.at[level, rows_of[c]],
+            sa_sem.at[to, c], ra_sem.at[level, c], slab=lax.max(j - 1 - to, 0),
         )
 
     def q_copy(level, to):
@@ -102,14 +110,20 @@
         with_q = base + 2 * half < slabs
         return half, sender, receiver, with_q
 
-    def send_own_a(level):
-        pack_for_send(send_a)
+    def send_a_chunk(level, c):
+        send_a[rows_of[c], :nb] = a_ref[rows_of[c], :].astype(BF16)
+        send_a[rows_of[c], nb:] = a_ref[imag_rows_of[c], :].astype(BF16)
         for to in range(1 << level):
-            a_copy(level, to).start()
-
-    pl.when(roles(0)[1])(lambda: send_own_a(0))
+            a_copy(level, to, c).start()
+
+    @pl.when(roles(0)[1])
+    def _():
+        for c in range(CHUNKS):
+            send_a_chunk(0, c)
 
     load_c.wait()
+    for load in small_loads:
+        load.wait()
 
     def set_q(q):
         high, low = split(q)
@@ -122,13 +136,13 @@
     @pl.when(j < slabs - 1)
     def _():
         gh, gl = split(a_ref[...])
-        size = nb // tiles.shape[1]
+        size = nb // tiles.shape[2]
         parts = []
         column = lax.broadcasted_iota(jnp.int32, (size, nb), 1) // size
-        for row in range(tiles.shape[1]):
-            hit = column == tiles[0, row, 0]
-            for other in range(1, tiles.shape[2]):
-                hit = jnp.logical_or(hit, column == tiles[0, row, other])
+        for row in range(tiles.shape[2]):
+            hit = column == tiles[0, 0, row]
+            for other in range(1, tiles.shape[0]):
+                hit = jnp.logical_or(hit, column == tiles[other, 0, row])
             rows = pl.ds(row * size, size)
             parts.append(jnp.where(hit, c_ref[rows, :], 0.0))
         ch, cl = split(jnp.concatenate(parts, axis=0))
@@ -139,9 +153,6 @@
 
         @pl.when(sender)
         def _():
-            if level > 0:
-                send_own_a(level)
-
             @pl.when(with_q)
             def _():
                 send_q[:, :nb] = qh[:nb, :]
@@ -151,13 +162,21 @@
 
         @pl.when(receiver)
         def _():
-            a_copy(level, 0).wait_recv()
-            beyond = got_a[level]
-            t_real, t_imag = fold(mm(qh[...], beyond) + mm(ql[...], beyond), nb)
-            th, tl = split(jnp.concatenate([t_real, t_imag], axis=0))
-            real, imag = fold(mm(th, qth[...]) + mm(tl, qth[...]) + mm(th, qtl[...]), nb)
-            a_ref[:nb, :] += real
-            a_ref[nb:, :] += imag
+            products = jnp.zeros((2 * nb, 2 * nb), F32)
+            for c in range(CHUNKS):
+                a_copy(level, 0, c).wait_recv()
+                beyond = got_a[level, rows_of[c]]
+                products += mm(qh[:, rows_of[c]], beyond) + mm(ql[:, rows_of[c]], beyond)
+            t_real, t_imag = fold(products, nb)
+            rows = nb // CHUNKS
+            for c in range(CHUNKS):
+                own = slice(c * rows, (c + 1) * rows)
+                th, tl = split(jnp.concatenate([t_real[own], t_imag[own]], axis=0))
+                last = mm(th, qth[...]) + mm(tl, qth[...]) + mm(th, qtl[...])
+                a_ref[rows_of[c], :] += last[:rows, :nb] - last[rows:, nb:]
+                a_ref[imag_rows_of[c], :] += last[:rows, nb:] + last[rows:, :nb]
+                if level + 1 < levels:
+                    pl.when(roles(level + 1)[1])(lambda: send_a_chunk(level + 1, c))
 
             @pl.when(with_q)
             def _():
@@ -174,8 +193,6 @@
     real, imag = a_ref[:nb, :], a_ref[nb:, :]
     mirrored = jnp.where(col < row, -real, imag).T
     packed[k] = (-occ[0] * (jnp.where(col > row, real, imag) + mirrored)).astype(BF16)
-
-    rows_of = [pl.ds(c * (nb // CHUNKS), nb // CHUNKS) for c in range(CHUNKS)]
 
     def to_right(q, c):
         block = packed.at[q, rows_of[c]]
@@ -277,7 +294,8 @@
         @pl.when(sender)
         def _():
             for to in range(half):
-                a_copy(level, to).wait_send()
+                for c in range(CHUNKS):
+                    a_copy(level, to, c).wait_send()
 
             @pl.when(with_q)
             def _():
@@ -303,7 +321,6 @@
     nb = coupling.shape[-1]
     levels = max((slabs - 1).bit_length(), 1)
     most = 1 << (levels - 1)
-    smem = pl.BlockSpec(memory_space=pltpu.SMEM)
     hbm = pl.BlockSpec(memory_space=pltpu.HBM)
     dma = pltpu.SemaphoreType.DMA
     green, self_energy = pl.pallas_call(
@@ -312,9 +329,13 @@
             jax.ShapeDtypeStruct((2 * nb, nb), F32),
             jax.ShapeDtypeStruct((2 * nb, nb), BF16),
         ),
-        in_specs=[hbm, hbm, smem, smem, smem, smem],
+        in_specs=[hbm] * 6,
         out_specs=(hbm, hbm),
         scratch_shapes=[
+            pltpu.SMEM(coupling_tiles.shape[2:] + coupling_tiles.shape[:2], jnp.int32),
+            pltpu.SMEM(occupation.shape, F32),
+            pltpu.SMEM(phonon_weight.shape, F32),
+            pltpu.SMEM(phonon_mode.shape, jnp.int32),
             pltpu.VMEM((2 * nb, nb), F32),
             pltpu.VMEM((nb, nb), F32),
             pltpu.VMEM((2 * nb, nb), BF16),
@@ -330,11 +351,11 @@
             pltpu.VMEM((nb, nb), F32),
             pltpu.VMEM((2, nb, nb), F32),
             pltpu.VMEM((2 * nb, nb), BF16),
+            dma((6,)),
             dma((2,)),
-            dma((2,)),
+            dma((most, CHUNKS)),
             dma((most,)),
-            dma((most,)),
-            dma((levels,)),
+            dma((levels, CHUNKS)),
             dma((levels,)),
             dma((momenta, CHUNKS)),
             dma((momenta, CHUNKS)),
@@ -343,12 +364,12 @@
             dma((2, CHUNKS)),
         ],
         compiler_params=pltpu.CompilerParams(
-            collective_id=0, has_side_effects=True, vmem_limit_bytes=40 * 1024 * 1024
+            collective_id=0, has_side_effects=True, vmem_limit_bytes=VMEM_BYTES
         ),
     )(
         free_green.reshape(2 * nb, nb),
         coupling.reshape(nb, nb),
-        coupling_tiles,
+        jnp.transpose(coupling_tiles, (2, 0, 1)),
         occupation,
         phonon_weight,
         phonon_mode,

time: 41.4 us -> 38.9 us (0.940)
  local copies, waits for them, and re-layouts: 4.81 us -> 2.62 us
    unnamed x13 -> x4, local copies, waits for them, and re-layouts: 4.81 us -> 2.62 us
where the time goes in v2:
time: 38.9 us; the launch traced here: 38.7 us
  Pallas kernels  34.8 us (89%)
  local copies, waits for them, and re-layouts  2.62 us (7%)
  between operations  1.29 us (3%)
    pallas_call x1, Pallas kernels, on_device(): pl.pallas_call(functools.partial(kernel, (slabs, momenta, energies, level...  34.8 us
    unnamed x4, local copies, waits for them, and re-layouts  2.62 us

profile of v2, /device:TPU:1, one launch (start us, length us, event | category | flops | bytes accessed | tf_op | source)
XLA Modules:
  0.0 38.7 jit_solution(16000557435283279775)
XLA Ops:
  1.3 34.8 %shard_map.77 = (f32[512,256]{1,0:T(8,128)}, bf16[512,256]{1,0:T(8,128)(2,1)}) custom-call(f32[512,256]{1,0:T(8,128)} %bitcast.5, f32[256,256]{1,0:T(8,128)} %bitcast.8, s32[3,1,8]{2,1,0:T(1,128)} %bitcast.9, f32[1]{0:T(128)S(6)} %copy.10.occ_hbm, f32[2,4,4]{2,1,0:T(4,128)} %weight_hbm.1, s32[2]{0:T(128)} %mode_hbm.1), custom_call_target="tpu_custom_call" | custom-call | tf_op jit(solution)/shard_map/pallas_call | solution.py:326
  36.1 0.0 copy-start
  36.1 1.9 %copy.11 = f32[1,1,1,2,256,256]{5,4,3,2,1,0:T(8,128)} copy(f32[1,1,1,2,256,256]{5,4,3,2,1,0:T(8,128)} %bitcast.6) | data formatting | bytes 1048576
  38.0 0.0 copy-done
  38.0 0.7 %copy.12 = bf16[1,1,1,2,256,256]{5,4,3,2,1,0:T(8,128)(2,1)} copy(bf16[1,1,1,2,256,256]{5,4,3,2,1,0:T(8,128)(2,1)S(1)} %bitcast.7) | data formatting | bytes 524288
Async XLA Ops:
  36.1 1.9 %copy-start = (bf16[512,256]{1,0:T(8,128)(2,1)S(1)}, bf16[512,256]{1,0:T(8,128)(2,1)}, u32[]{:S(2)}) copy-start(bf16[512,256]{1,0:T(8,128)(2,1)} %get-tuple-element.5) | copy-start | bytes 786436

commit v3 on v2

--- a/solution.py
+++ b/solution.py
@@ -10,6 +10,7 @@
 F32 = jnp.float32
 BF16 = jnp.bfloat16
 CHUNKS = 2
+RELAYS = 4
 VMEM_BYTES = 62 * 1024 * 1024
 
 
@@ -162,17 +163,23 @@
 
         @pl.when(receiver)
         def _():
-            products = jnp.zeros((2 * nb, 2 * nb), F32)
+            products = 0.0
             for c in range(CHUNKS):
                 a_copy(level, 0, c).wait_recv()
                 beyond = got_a[level, rows_of[c]]
-                products += mm(qh[:, rows_of[c]], beyond) + mm(ql[:, rows_of[c]], beyond)
+                products += mm(
+                    jnp.concatenate([qh[:, rows_of[c]], ql[:, rows_of[c]]], axis=1),
+                    jnp.concatenate([beyond, beyond], axis=0),
+                )
             t_real, t_imag = fold(products, nb)
             rows = nb // CHUNKS
             for c in range(CHUNKS):
                 own = slice(c * rows, (c + 1) * rows)
                 th, tl = split(jnp.concatenate([t_real[own], t_imag[own]], axis=0))
-                last = mm(th, qth[...]) + mm(tl, qth[...]) + mm(th, qtl[...])
+                last = mm(
+                    jnp.concatenate([th, tl, th], axis=1),
+                    jnp.concatenate([qth[...], qth[...], qtl[...]], axis=0),
+                )
                 a_ref[rows_of[c], :] += last[:rows, :nb] - last[rows:, nb:]
                 a_ref[imag_rows_of[c], :] += last[:rows, nb:] + last[rows:, :nb]
                 if level + 1 < levels:
@@ -194,15 +201,17 @@
     mirrored = jnp.where(col < row, -real, imag).T
     packed[k] = (-occ[0] * (jnp.where(col > row, real, imag) + mirrored)).astype(BF16)
 
+    part_of = [pl.ds(c * (nb // RELAYS), nb // RELAYS) for c in range(RELAYS)]
+
     def to_right(q, c):
-        block = packed.at[q, rows_of[c]]
+        block = packed.at[q, part_of[c]]
         return remote(
             block, block, right_sem.at[q, c], block_sem.at[q, c],
             kmom=lax.min(k + 1, momenta - 1),
         )
 
     def to_left(q, c):
-        block = packed.at[q, rows_of[c]]
+        block = packed.at[q, part_of[c]]
         return remote(
             block, block, left_sem.at[q, c], block_sem.at[q, c], kmom=lax.max(k - 1, 0)
         )
@@ -210,14 +219,14 @@
     def near_copy(side, c):
         target = lax.min(e + 1, energies - 1) if side == 0 else lax.max(e - 1, 0)
         return remote(
-            sum1.at[rows_of[c]], near.at[side, rows_of[c]],
+            sum1.at[part_of[c]], near.at[side, part_of[c]],
             es_sem.at[side, c], er_sem.at[side, c], energy=target,
         )
 
     has_right, has_left = k < momenta - 1, k > 0
     has_next, has_before = e < energies - 1, e > 0
 
-    for c in range(CHUNKS):
+    for c in range(RELAYS):
         pl.when(has_right)(lambda: to_right(k, c).start())
         pl.when(has_left)(lambda: to_left(k, c).start())
 
@@ -230,20 +239,20 @@
         return w0, w1
 
     own0, own1 = weights(k)
-    for c in range(CHUNKS):
-        block = packed[k, rows_of[c]].astype(F32)
-        sum0[rows_of[c]] = own0 * block
-        sum1[rows_of[c]] = own1 * block
+    for c in range(RELAYS):
+        block = packed[k, part_of[c]].astype(F32)
+        sum0[part_of[c]] = own0 * block
+        sum1[part_of[c]] = own1 * block
 
     def take(q, c):
         w0, w1 = weights(q)
-        block = packed[q, rows_of[c]].astype(F32)
-        sum1[rows_of[c]] += w1 * block
-        sum0[rows_of[c]] += w0 * block
+        block = packed[q, part_of[c]].astype(F32)
+        sum1[part_of[c]] += w1 * block
+        sum0[part_of[c]] += w0 * block
 
     for step in range(1, momenta):
         low, high = k - step, k + step
-        for c in range(CHUNKS):
+        for c in range(RELAYS):
 
             @pl.when(low >= 0)
             def _():
@@ -263,21 +272,21 @@
                 pl.when(has_next)(lambda: near_copy(0, c).start())
                 pl.when(has_before)(lambda: near_copy(1, c).start())
     if momenta == 1:
-        for c in range(CHUNKS):
+        for c in range(RELAYS):
             pl.when(has_next)(lambda: near_copy(0, c).start())
             pl.when(has_before)(lambda: near_copy(1, c).start())
 
-    for c in range(CHUNKS):
+    for c in range(RELAYS):
 
         @pl.when(has_before)
         def _():
             near_copy(0, c).wait_recv()
-            sum0[rows_of[c]] += near[0, rows_of[c]]
+            sum0[part_of[c]] += near[0, part_of[c]]
 
         @pl.when(has_next)
         def _():
             near_copy(1, c).wait_recv()
-            sum0[rows_of[c]] += near[1, rows_of[c]]
+            sum0[part_of[c]] += near[1, part_of[c]]
 
     total = sum0[...]
     turned = total.T
@@ -302,7 +311,7 @@
                 for to in range(half):
                     q_copy(level, to).wait_send()
 
-    for c in range(CHUNKS):
+    for c in range(RELAYS):
         for q in range(momenta):
             pl.when(jnp.logical_and(has_right, q <= k))(
                 lambda: to_right(q, c).wait_send()
@@ -321,7 +330,7 @@
     nb = coupling.shape[-1]
     levels = max((slabs - 1).bit_length(), 1)
     most = 1 << (levels - 1)
-    hbm = pl.BlockSpec(memory_space=pltpu.HBM)
+    hbm = pl.BlockSpec(memory_space=pl.ANY)
     dma = pltpu.SemaphoreType.DMA
     green, self_energy = pl.pallas_call(
         functools.partial(kernel, (slabs, momenta, energies, levels)),
@@ -357,11 +366,11 @@
             dma((most,)),
             dma((levels, CHUNKS)),
             dma((levels,)),
-            dma((momenta, CHUNKS)),
-            dma((momenta, CHUNKS)),
-            dma((momenta, CHUNKS)),
-            dma((2, CHUNKS)),
-            dma((2, CHUNKS)),
+            dma((momenta, RELAYS)),
+            dma((momenta, RELAYS)),
+            dma((momenta, RELAYS)),
+            dma((2, RELAYS)),
+            dma((2, RELAYS)),
         ],
         compiler_params=pltpu.CompilerParams(
             collective_id=0, has_side_effects=True, vmem_limit_bytes=VMEM_BYTES

time: 38.9 us -> 38.2 us (0.982)
  Pallas kernels: 34.8 us -> 34.1 us
    pallas_call x1, Pallas kernels: 34.8 us -> 34.1 us  [on_device(): pl.pallas_call(functools.partial(kernel, (slabs, momenta, energies, level...]
where the time goes in v3:
time: 38.2 us; the launch traced here: 38 us
  Pallas kernels  34.1 us (89%)
  local copies, waits for them, and re-layouts  2.62 us (7%)
  between operations  1.29 us (3%)
    pallas_call x1, Pallas kernels, on_device(): pl.pallas_call(functools.partial(kernel, (slabs, momenta, energies, level...  34.1 us
    unnamed x4, local copies, waits for them, and re-layouts  2.62 us

profile of v3, /device:TPU:1, one launch (start us, length us, event | category | flops | bytes accessed | tf_op | source)
XLA Modules:
  0.0 38.0 jit_solution(17981632859724709272)
XLA Ops:
  1.3 34.1 %shard_map.77 = (f32[512,256]{1,0:T(8,128)}, bf16[512,256]{1,0:T(8,128)(2,1)}) custom-call(f32[512,256]{1,0:T(8,128)} %bitcast.5, f32[256,256]{1,0:T(8,128)} %bitcast.8, s32[3,1,8]{2,1,0:T(1,128)} %bitcast.9, f32[1]{0:T(128)S(6)} %copy.10.occ_hbm, f32[2,4,4]{2,1,0:T(4,128)} %weight_hbm.1, s32[2]{0:T(128)} %mode_hbm.1), custom_call_target="tpu_custom_call" | custom-call | tf_op jit(solution)/shard_map/pallas_call | solution.py:335
  35.4 0.0 copy-start
  35.4 1.9 %copy.11 = f32[1,1,1,2,256,256]{5,4,3,2,1,0:T(8,128)} copy(f32[1,1,1,2,256,256]{5,4,3,2,1,0:T(8,128)} %bitcast.6) | data formatting | bytes 1048576
  37.3 0.0 copy-done
  37.3 0.7 %copy.12 = bf16[1,1,1,2,256,256]{5,4,3,2,1,0:T(8,128)(2,1)} copy(bf16[1,1,1,2,256,256]{5,4,3,2,1,0:T(8,128)(2,1)S(1)} %bitcast.7) | data formatting | bytes 524288
Async XLA Ops:
  35.4 1.9 %copy-start = (bf16[512,256]{1,0:T(8,128)(2,1)S(1)}, bf16[512,256]{1,0:T(8,128)(2,1)}, u32[]{:S(2)}) copy-start(bf16[512,256]{1,0:T(8,128)(2,1)} %get-tuple-element.5) | copy-start | bytes 786436
